TPU v7x, 32 devices: a whole 2x2x4 slice. The times are simulated.
32 devices in a mesh: pp: 4 (over y, core), ep: 8 (over z, x).
Axes of the slice: x: 2, y: 2, z: 4, core: 2. Of those that a mesh axis runs over, the one named last changes fastest.
Arguments:
- fwd_tokens: bfloat16 [4, 1024, 3584], P('pp', 'ep'), may hold values from -6 to 6
- fwd_routes: int32 [4, 1024, 2], P('pp', 'ep'), may hold values from 0 to 3, all different within a row; in each aligned block of 128 rows (0 to 127, 128 to 255, ..., all dimensions but the last counted through in order) at most 96 rows name the same one
- fwd_weights: float32 [4, 1024, 2], P('pp', 'ep'), may hold values from 0.2 to 1
- bwd_tokens: bfloat16 [4, 1024, 3584], P('pp', 'ep'), may hold values from -6 to 6
- bwd_grads: bfloat16 [4, 1024, 3584], P('pp', 'ep'), may hold values from -6 to 6
- bwd_routes: int32 [4, 1024, 2], P('pp', 'ep'), may hold values from 0 to 3, all different within a row; in each aligned block of 128 rows (0 to 127, 128 to 255, ..., all dimensions but the last counted through in order) at most 96 rows name the same one
- bwd_weights: float32 [4, 1024, 2], P('pp', 'ep'), may hold values from 0.2 to 1
- up_proj: bfloat16 [4, 3584, 4096], P('pp', None, 'ep'), may hold values from -0.09375 to 0.09375
- down_proj: bfloat16 [4, 4096, 3584], P('pp', 'ep'), may hold values from -0.1875 to 0.1875
Outputs:
- next_input: bfloat16 [4, 1024, 3584], P('pp', 'ep')
- prev_grad: bfloat16 [4, 1024, 3584], P('pp', 'ep')
Inputs may be any that keep to these rules, and one draw needn't show every extreme that they name: `fwd_routes`: each row names 2 different experts. Among the 128 rows of one device no expert is named more than 96 times; on some devices some expert is named exactly 96 times. `bwd_routes`: as for fwd_routes.
All inputs are finite; a program needn't handle non-finite values.
Results may differ from a plain program's by a relative error of at most 0.0043.
Values may be sent and summed in bfloat16 or wider, within the bound.
A program may use at most 128 MiB of HBM per device.

v0:
```python
import jax
import jax.numpy as jnp
from jax import lax
from jax.sharding import PartitionSpec as P


def as_sent(value):

    def short(part):
        return part.astype(jnp.bfloat16) if part.dtype == jnp.float32 else part

    return jax.tree.map(short, value)


def from_behind(value, axis, by):
    size = lax.axis_size(axis)
    return lax.ppermute(value, axis, [(i, (i + by) % size) for i in range(size)])


def silu_slope(pre_act):
    sigmoid_value = jax.nn.sigmoid(pre_act)
    return sigmoid_value * (1.0 + pre_act * (1.0 - sigmoid_value))


def slot_numbers(routes, expert_count, capacity):
    chosen = routes[0]
    tok_rows, route_count = chosen.shape
    onehot = (
        chosen[:, :, None] == jnp.arange(expert_count, dtype=jnp.int32)[None, None, :]
    ).astype(jnp.int32)
    flat_hot = onehot.reshape(tok_rows * route_count, expert_count)
    earlier = jnp.cumsum(flat_hot, axis=0) - flat_hot
    position = jnp.sum(earlier * flat_hot, axis=1).reshape(tok_rows, route_count)
    return chosen * capacity + position


def pack_rows(sources, slots, slot_total):
    slot_table = jnp.sum(
        (slots[:, :, None] == jnp.arange(slot_total, dtype=jnp.int32)[None, None, :]).astype(
            jnp.bfloat16
        ),
        axis=1,
    )
    return tuple(
        (
            lax.dot_general(
                slot_table, member, (((0,), (0,)), ((), ())), preferred_element_type=jnp.float32
            ).astype(jnp.bfloat16)
            for member in sources
        )
    )


def combine_rows(residual, results, slots, route_weights):
    picked = results[slots].astype(jnp.float32)
    combined = residual.astype(jnp.float32) + jnp.sum(route_weights[:, :, None] * picked, axis=1)
    return combined.astype(jnp.bfloat16)


def forward_work(received, w_up, w_down):
    hidden = jax.nn.silu(
        jnp.einsum("scd,df->scf", received[0], w_up, preferred_element_type=jnp.float32)
    ).astype(jnp.bfloat16)
    return (jnp.einsum("scf,fd->scd", hidden, w_down, preferred_element_type=jnp.float32),)


def backward_work(received, w_up, w_down):
    pre_act = jnp.einsum("scd,df->scf", received[0], w_up, preferred_element_type=jnp.float32)
    upstream = jnp.einsum("scd,fd->scf", received[1], w_down, preferred_element_type=jnp.float32)
    hidden_grad = (silu_slope(pre_act) * upstream).astype(jnp.bfloat16)
    return (jnp.einsum("scf,df->scd", hidden_grad, w_up, preferred_element_type=jnp.float32),)


def pair_duplicate(outgoing, expert_work, expert_count, feature_count):

    def handle(received):
        partials = expert_work(received)
        rounded = tuple((member.astype(jnp.bfloat16) for member in partials))
        return jax.tree.map(
            lambda part, own: part.astype(own.dtype),
            lax.all_to_all(as_sent(rounded), "ep", split_axis=0, concat_axis=0, tiled=True),
            rounded,
        )

    returned = handle(
        jax.tree.map(
            lambda part, own: part.astype(own.dtype),
            lax.all_to_all(as_sent(outgoing), "ep", split_axis=0, concat_axis=0, tiled=True),
            outgoing,
        )
    )
    results = []
    for member in returned:
        paired = member.reshape(expert_count, 2, member.shape[1], feature_count).astype(jnp.float32)
        results.append(jnp.sum(paired, axis=1).astype(jnp.bfloat16).reshape(-1, feature_count))
    return tuple(results)


def on_device(
    fwd_tokens,
    fwd_routes,
    fwd_weights,
    bwd_tokens,
    bwd_grads,
    bwd_routes,
    bwd_weights,
    up_proj,
    down_proj,
):
    ep_count = lax.axis_size("ep")
    expert_count = ep_count // 2
    tok_rows = fwd_tokens.shape[1]
    feature_count = fwd_tokens.shape[2]
    route_count = fwd_routes.shape[2]
    capacity = 3 * tok_rows * route_count // ep_count
    slot_total = expert_count * capacity
    w_up = up_proj[0]
    w_down = down_proj[0]
    fwd_slots = slot_numbers(fwd_routes, expert_count, capacity)
    bwd_slots = slot_numbers(bwd_routes, expert_count, capacity)
    fwd_packed = pack_rows((fwd_tokens[0],), fwd_slots, slot_total)
    bwd_packed = pack_rows((bwd_tokens[0], bwd_grads[0]), bwd_slots, slot_total)

    def forward_fn(received):
        return forward_work(received, w_up, w_down)

    def backward_fn(received):
        return backward_work(received, w_up, w_down)

    def layout(packed):
        spread = []
        for member in packed:
            copies = jnp.broadcast_to(
                member.reshape(expert_count, 1, capacity, feature_count),
                (expert_count, 2, capacity, feature_count),
            )
            spread.append(copies.reshape(ep_count, capacity, feature_count))
        return tuple(spread)

    (fwd_results,) = pair_duplicate(layout(fwd_packed), forward_fn, expert_count, feature_count)
    (bwd_results,) = pair_duplicate(layout(bwd_packed), backward_fn, expert_count, feature_count)
    fwd_out = combine_rows(fwd_tokens[0], fwd_results, fwd_slots, fwd_weights[0])
    bwd_out = combine_rows(bwd_grads[0], bwd_results, bwd_slots, bwd_weights[0])
    next_input = from_behind(fwd_out[None], "pp", 1)
    prev_grad = from_behind(bwd_out[None], "pp", -1)
    return (next_input, prev_grad)


def solution(mesh):
    placed = (
        P("pp", "ep", None),
        P("pp", "ep", None),
        P("pp", "ep", None),
        P("pp", "ep", None),
        P("pp", "ep", None),
        P("pp", "ep", None),
        P("pp", "ep", None),
        P("pp", None, "ep"),
        P("pp", "ep", None),
    )
    return jax.shard_map(
        on_device,
        mesh=mesh,
        in_specs=placed,
        out_specs=(P("pp", "ep", None), P("pp", "ep", None)),
        check_vma=False,
    )
```

profile of v0, /device:TPU:0, one launch (start us, length us, event | category | flops | bytes accessed | tf_op | source)
XLA Modules:
  0.0 678.6 jit_solution(12247291913912465651)
XLA Ops:
  0.6 0.0 copy-start
  0.6 0.9 copy.39
  1.5 0.1 eq.93
  1.7 0.1 eq.89
  1.8 1.2 reduce-window.16
  3.0 0.1 slice.21
  3.1 0.1 copy.42
  3.3 0.1 copy.43
  3.4 0.1 add_bitcast_fusion
  3.4 0.1 reshape.166
  3.6 0.1 copy.44
  3.7 0.1 fusion.23
  3.8 0.9 convolution_convert_fusion.3
  4.7 2.9 broadcast_in_dim.15
  7.6 7.3 %all-to-all-start.2 = ((bf16[8,96,3584]{2,1,0:T(8,128)(2,1)}), bf16[8,96,3584]{2,1,0:T(8,128)(2,1)}, u32[]{:S(2)}, u32[]{:S(2)}) async-start(bf16[8,96,3584]{2,1,0:T(8,128)(2,1)} %bitcast.117), calls=%async_computation.2 | async-start | bytes 11010048 | tf_op jit(solution)/shard_map/all_to_all | solution.py:88
  14.9 2.1 convolution_convert_fusion.2
  17.0 119.3 %all-to-all-done.2 = bf16[8,96,3584]{2,1,0:T(8,128)(2,1)} async-done(((bf16[8,96,3584]{2,1,0:T(8,128)(2,1)}), bf16[8,96,3584]{2,1,0:T(8,128)(2,1)}, u32[]{:S(2)}, u32[]{:S(2)}) %all-to-all-start.2) | async-done | bytes 5505056 | tf_op jit(solution)/shard_map/all_to_all | solution.py:88
  136.3 2.9 broadcast_in_dim.17
  139.2 4.8 all-to-all-start.3
  144.0 0.1 copy.32
  144.1 0.1 eq.82
  144.3 0.1 eq.78
  144.4 1.2 reduce-window.14
  145.7 0.1 slice.20
  145.7 0.1 copy.35
  145.9 0.1 copy.36
  146.0 0.1 add_bitcast_fusion.1
  146.1 0.1 reshape.160
  146.2 0.1 copy.37
  146.3 0.1 fusion.24
  146.4 2.1 convolution_convert_fusion.4
  148.5 116.0 %all-to-all-done.3 = bf16[8,96,3584]{2,1,0:T(8,128)(2,1)} async-done(((bf16[8,96,3584]{2,1,0:T(8,128)(2,1)}), bf16[8,96,3584]{2,1,0:T(8,128)(2,1)}, u32[]{:S(2)}, u32[]{:S(2)}) %all-to-all-start.3) | async-done | bytes 5505056 | tf_op jit(solution)/shard_map/all_to_all | solution.py:88
  264.5 2.9 broadcast_in_dim.13
  267.4 4.7 all-to-all-start
  272.1 6.1 fusion.4
  278.2 13.2 %convolution_convert_fusion = bf16[8,96,3584]{2,1,0:T(8,128)(2,1)} fusion(bf16[1,3584,512]{2,1,0:T(8,128)(2,1)} %param.16, f32[8,96,512]{2,1,0:T(8,128)S(1)} %fusion.4, bf16[8,96,3584]{2,1,0:T(8,128)(2,1)} %all-to-all-done.3, bf16[1,512,3584]{2,1,0:T(8,128)(2,1)} %param.17), kind=kOutput, calls=%fused_computation.2 | convolution fusion | flops 5643436032 | bytes 19922944 | tf_op jit(solution)/shard_map/scf,df->scd/dot_general | solution.py:71
  291.4 101.2 %all-to-all-done = bf16[8,96,3584]{2,1,0:T(8,128)(2,1)} async-done(((bf16[8,96,3584]{2,1,0:T(8,128)(2,1)}), bf16[8,96,3584]{2,1,0:T(8,128)(2,1)}, u32[]{:S(2)}, u32[]{:S(2)}) %all-to-all-start) | async-done | bytes 5505056 | tf_op jit(solution)/shard_map/all_to_all | solution.py:88
  392.6 4.9 all-to-all-start.4
  397.5 13.1 %convolution_convert_fusion.1 = bf16[8,96,3584]{2,1,0:T(8,128)(2,1)} fusion(bf16[1,512,3584]{2,1,0:T(8,128)(2,1)} %param.17, bf16[8,96,3584]{2,1,0:T(8,128)(2,1)} %all-to-all-done, bf16[1,3584,512]{2,1,0:T(8,128)(2,1)} %param.16), kind=kOutput, calls=%fused_computation.3 | convolution fusion | flops 5641863168 | bytes 18350080 | tf_op jit(solution)/shard_map/scf,fd->scd/dot_general | solution.py:64
  410.6 107.2 %all-to-all-done.4 = bf16[8,96,3584]{2,1,0:T(8,128)(2,1)} async-done(((bf16[8,96,3584]{2,1,0:T(8,128)(2,1)}), bf16[8,96,3584]{2,1,0:T(8,128)(2,1)}, u32[]{:S(2)}, u32[]{:S(2)}) %all-to-all-start.4) | async-done | bytes 5505056 | tf_op jit(solution)/shard_map/all_to_all | solution.py:81
  517.9 4.7 all-to-all-start.1
  522.6 0.1 reshape.171
  522.7 0.1 reshape.164
  522.9 0.1 reshape.182
  523.0 0.1 copy.38
  523.2 0.1 reshape.174
  523.3 0.1 copy.31
  523.5 3.8 bitcast_reduce_fusion
  527.3 3.0 gather_fusion.1
  530.3 5.2 reshape.191
  535.4 7.4 %multiply_reduce_fusion = f32[128,3584]{1,0:T(8,128)S(1)} fusion(f32[128,2,3584]{2,1,0:T(2,128)} %reshape.191, f32[128,2]{1,0:T(8,128)S(1)} %copy.38), kind=kLoop, calls=%fused_computation.17 | loop fusion | flops 1376256 | bytes 5506048 | tf_op jit(solution)/shard_map/reduce_sum | solution.py:56
  542.9 1.1 fusion.8
  543.9 0.0 collective-permute-start.1
  543.9 99.1 %all-to-all-done.1 = bf16[8,96,3584]{2,1,0:T(8,128)(2,1)} async-done(((bf16[8,96,3584]{2,1,0:T(8,128)(2,1)}), bf16[8,96,3584]{2,1,0:T(8,128)(2,1)}, u32[]{:S(2)}, u32[]{:S(2)}) %all-to-all-start.1) | async-done | bytes 5505056 | tf_op jit(solution)/shard_map/all_to_all | solution.py:81
  643.0 3.8 bitcast_reduce_fusion.1
  646.9 3.0 gather_fusion
  649.9 5.2 reshape.190
  655.1 7.5 %multiply_reduce_fusion.1 = f32[128,3584]{1,0:T(8,128)S(1)} fusion(f32[128,2,3584]{2,1,0:T(2,128)} %reshape.190, f32[128,2]{1,0:T(8,128)S(1)} %copy.31), kind=kLoop, calls=%fused_computation.18 | loop fusion | flops 1376256 | bytes 5506048 | tf_op jit(solution)/shard_map/reduce_sum | solution.py:56
  662.5 0.2 fusion.9
  662.7 0.1 collective-permute-start
  662.8 0.0 collective-permute-done.1
  662.8 12.8 %collective-permute-done = bf16[1,128,3584]{2,1,0:T(8,128)(2,1)S(1)} collective-permute-done((bf16[1,128,3584]{2,1,0:T(8,128)(2,1)S(1)}, bf16[1,128,3584]{2,1,0:T(8,128)(2,1)S(1)}, u32[]{:S(2)}, u32[]{:S(2)}) %collective-permute-start) | collective-permute-done | bytes 917536 | tf_op jit(solution)/shard_map/ppermute | solution.py:17
  675.6 0.9 copy.51
  676.5 2.2 copy.52
  (27 shorter events, 0.2 us)
Async XLA Ops:
  0.6 3.2 copy-start
  7.6 128.6 %all-to-all-start.2 = ((bf16[8,96,3584]{2,1,0:T(8,128)(2,1)}), bf16[8,96,3584]{2,1,0:T(8,128)(2,1)}, u32[]{:S(2)}, u32[]{:S(2)}) async-start(bf16[8,96,3584]{2,1,0:T(8,128)(2,1)} %bitcast.117), calls=%async_computation.2 | async-start | bytes 11010048 | tf_op jit(solution)/shard_map/all_to_all | solution.py:88
  139.2 4.8 copy-start.4
  139.2 125.3 %all-to-all-start.3 = ((bf16[8,96,3584]{2,1,0:T(8,128)(2,1)}), bf16[8,96,3584]{2,1,0:T(8,128)(2,1)}, u32[]{:S(2)}, u32[]{:S(2)}) async-start(bf16[8,96,3584]{2,1,0:T(8,128)(2,1)} %bitcast.115), calls=%async_computation.3 | async-start | bytes 11010048 | tf_op jit(solution)/shard_map/all_to_all | solution.py:88
  267.4 125.2 %all-to-all-start = ((bf16[8,96,3584]{2,1,0:T(8,128)(2,1)}), bf16[8,96,3584]{2,1,0:T(8,128)(2,1)}, u32[]{:S(2)}, u32[]{:S(2)}) async-start(bf16[8,96,3584]{2,1,0:T(8,128)(2,1)} %bitcast.116), calls=%async_computation | async-start | bytes 11010048 | tf_op jit(solution)/shard_map/all_to_all | solution.py:88
  392.6 125.3 %all-to-all-start.4 = ((bf16[8,96,3584]{2,1,0:T(8,128)(2,1)}), bf16[8,96,3584]{2,1,0:T(8,128)(2,1)}, u32[]{:S(2)}, u32[]{:S(2)}) async-start(bf16[8,96,3584]{2,1,0:T(8,128)(2,1)} %convolution_convert_fusion), calls=%async_computation.4 | async-start | bytes 11010048 | tf_op jit(solution)/shard_map/all_to_all | solution.py:81
  410.6 112.4 %copy-start.5 = (f32[1,128,2]{1,2,0:T(2,128)S(1)}, f32[1,128,2]{1,2,0:T(2,128)}, u32[]{:S(2)}) copy-start(f32[1,128,2]{1,2,0:T(2,128)} %param.15) | copy-start | bytes 3076
  410.6 112.7 %copy-start.6 = (f32[1,128,2]{1,2,0:T(2,128)S(1)}, f32[1,128,2]{1,2,0:T(2,128)}, u32[]{:S(2)}) copy-start(f32[1,128,2]{1,2,0:T(2,128)} %param.11) | copy-start | bytes 3076
  517.9 125.2 %all-to-all-start.1 = ((bf16[8,96,3584]{2,1,0:T(8,128)(2,1)}), bf16[8,96,3584]{2,1,0:T(8,128)(2,1)}, u32[]{:S(2)}, u32[]{:S(2)}) async-start(bf16[8,96,3584]{2,1,0:T(8,128)(2,1)} %convolution_convert_fusion.1), calls=%async_computation.1 | async-start | bytes 11010048 | tf_op jit(solution)/shard_map/all_to_all | solution.py:81
  535.4 7.4 %copy-start.2 = (bf16[1,128,3584]{2,1,0:T(8,128)(2,1)S(1)}, bf16[1,128,3584]{2,1,0:T(8,128)(2,1)}, u32[]{:S(2)}) copy-start(bf16[1,128,3584]{2,1,0:T(8,128)(2,1)} %param.13) | copy-start | bytes 2752516
  543.9 118.8 %collective-permute-start.1 = (bf16[1,128,3584]{2,1,0:T(8,128)(2,1)}, bf16[1,128,3584]{2,1,0:T(8,128)(2,1)}, u32[]{:S(2)}, u32[]{:S(2)}) collective-permute-start(bf16[1,128,3584]{2,1,0:T(8,128)(2,1)} %fusion.8), channel_id=1, source_target_pairs={{0,24},{8,0},{16,8},{24,16},{1,25},{9,1},{17,9},{25,17},{2,26},{10... | collective-permute-start | bytes 2752520 | tf_op jit(solution)/shard_map/ppermute | solution.py:17
  655.1 7.5 %copy-start.3 = (bf16[1,128,3584]{2,1,0:T(8,128)(2,1)S(1)}, bf16[1,128,3584]{2,1,0:T(8,128)(2,1)}, u32[]{:S(2)}) copy-start(bf16[1,128,3584]{2,1,0:T(8,128)(2,1)} %param.9) | copy-start | bytes 2752516
  655.1 23.6 %copy-start.1 = (bf16[1,128,3584]{2,1,0:T(8,128)(2,1)S(1)}, bf16[1,128,3584]{2,1,0:T(8,128)(2,1)}, u32[]{:S(2)}) copy-start(bf16[1,128,3584]{2,1,0:T(8,128)(2,1)} %param.12) | copy-start | bytes 2752516
  662.7 12.9 %collective-permute-start = (bf16[1,128,3584]{2,1,0:T(8,128)(2,1)S(1)}, bf16[1,128,3584]{2,1,0:T(8,128)(2,1)S(1)}, u32[]{:S(2)}, u32[]{:S(2)}) collective-permute-start(bf16[1,128,3584]{2,1,0:T(8,128)(2,1)S(1)} %fusion.9), channel_id=1, source_target_pairs={{0,8},{8,16},{16,24},{24,0},{1,9},{9,17},{17,25},{25,1},{2,10},{10... | collective-permute-start | bytes 2752520 | tf_op jit(solution)/shard_map/ppermute | solution.py:17
where the time goes:
time: 680 us; the launch traced here: 679 us
  waiting for transfers between devices  556 us (82%)
  matrix products  37.5 us (6%)
  local copies, waits for them, and re-layouts  31.4 us (5%)
  other arithmetic  26.8 us (4%)
  starting transfers between devices  26.4 us (4%)
    all_to_all x3, waiting for transfers between devices, pair_duplicate(): lax.all_to_all(as_sent(outgoing), 'ep', split_axis=0, concat_axis=0, tile...  336 us
    all_to_all x2, waiting for transfers between devices, handle(): lax.all_to_all(as_sent(rounded), 'ep', split_axis=0, concat_axis=0, tiled...  206 us
    all_to_all x3, starting transfers between devices, pair_duplicate(): lax.all_to_all(as_sent(outgoing), 'ep', split_axis=0, concat_axis=0, tile...  16.8 us
    reduce_sum x2, other arithmetic, combine_rows(): jnp.sum(route_weights[:, :, None] * picked, axis=1)  14.8 us
  transfers between devices with their start and end apart: 7, of which 6 were waited for; matrix products, arithmetic and copies ran while one was open for 12% of the time, Pallas kernels for 0%

commit v1 on v0

v1 whole, which is shorter than its diff:
```python
import functools

import jax
import jax.numpy as jnp
from jax import lax
from jax.experimental import pallas as pl
from jax.experimental.pallas import tpu as pltpu
from jax.sharding import PartitionSpec as P

MESH = pl.DeviceIdType.MESH
NT = (((1,), (1,)), ((), ()))
NN = (((1,), (0,)), ((), ()))


def from_behind(value, axis, by):
    size = lax.axis_size(axis)
    return lax.ppermute(value, axis, [(i, (i + by) % size) for i in range(size)])


def silu_slope(pre_act):
    sigmoid_value = jax.nn.sigmoid(pre_act)
    return sigmoid_value * (1.0 + pre_act * (1.0 - sigmoid_value))


def slot_numbers(routes, expert_count, capacity):
    chosen = routes[0]
    tok_rows, route_count = chosen.shape
    onehot = (
        chosen[:, :, None] == jnp.arange(expert_count, dtype=jnp.int32)[None, None, :]
    ).astype(jnp.int32)
    flat_hot = onehot.reshape(tok_rows * route_count, expert_count)
    earlier = jnp.cumsum(flat_hot, axis=0) - flat_hot
    position = jnp.sum(earlier * flat_hot, axis=1).reshape(tok_rows, route_count)
    return chosen * capacity + position


def pack_rows(sources, slots, slot_total):
    slot_table = jnp.sum(
        (slots[:, :, None] == jnp.arange(slot_total, dtype=jnp.int32)[None, None, :]).astype(
            jnp.bfloat16
        ),
        axis=1,
    )
    return tuple(
        lax.dot_general(
            slot_table, member, (((0,), (0,)), ((), ())), preferred_element_type=jnp.float32
        ).astype(jnp.bfloat16)
        for member in sources
    )


def combine_rows(residual, results, slots, route_weights):
    slot_total = results.shape[0]
    hot = slots[:, :, None] == jnp.arange(slot_total, dtype=jnp.int32)[None, None, :]
    table = jnp.sum(jnp.where(hot, route_weights[:, :, None], 0.0), axis=1)
    high = lax.reduce_precision(table, 8, 7)
    both = jnp.concatenate([high.astype(jnp.bfloat16), (table - high).astype(jnp.bfloat16)], axis=0)
    sums = jnp.dot(both, results, preferred_element_type=jnp.float32)
    rows = residual.shape[0]
    return (residual.astype(jnp.float32) + sums[:rows] + sums[rows:]).astype(jnp.bfloat16)


def relay_kernel(
    experts, f_in, x_in, g_in, up_ref, down_ref, f_out, b_out,
    f_rows, x_rows, g_rows, f_part, b_part, f_other, b_other,
    z_send, z_recv, l_sem, x_send, x_recv, xr_send, xr_recv, zr_send, zr_recv, lr_sem,
):
    me = lax.axis_index("ep")
    mine = me // 2
    half = lax.rem(me, 2)
    partner = 2 * mine + 1 - half
    capacity, width = f_in.shape[1], f_in.shape[2]
    piece = 512 if width % 512 == 0 else 128
    pieces = width // piece
    hidden_size = up_ref.shape[1]

    def ahead(k):
        return lax.rem(mine + k, experts)

    def behind(k):
        return lax.rem(mine + experts - k, experts)

    barrier = pltpu.get_barrier_semaphore()
    pl.semaphore_signal(barrier, inc=1, device_id={"ep": partner}, device_id_type=MESH)
    for k in range(1, experts):
        pl.semaphore_signal(
            barrier, inc=1, device_id={"ep": 2 * ahead(k) + half}, device_id_type=MESH
        )
    pl.semaphore_wait(barrier, experts)

    ins = (f_in, x_in, g_in)
    rows = (f_rows, x_rows, g_rows)
    parts = (f_part, b_part)
    others = (f_other, b_other)
    outs = (f_out, b_out)

    def along(a, k):
        return pltpu.make_async_remote_copy(
            src_ref=ins[a].at[ahead(k)], dst_ref=rows[a].at[k, 0],
            send_sem=z_send.at[a, k], recv_sem=z_recv.at[a, k],
            device_id={"ep": 2 * ahead(k) + half}, device_id_type=MESH,
        )

    def own(a):
        return pltpu.make_async_copy(ins[a].at[mine], rows[a].at[0, 0], l_sem.at[a])

    def across(a, k):
        return pltpu.make_async_remote_copy(
            src_ref=ins[a].at[mine] if k == 0 else rows[a].at[k, 0], dst_ref=rows[a].at[k, 1],
            send_sem=x_send.at[a, k], recv_sem=x_recv.at[a, k],
            device_id={"ep": partner}, device_id_type=MESH,
        )

    def back_across(a, k):
        return pltpu.make_async_remote_copy(
            src_ref=parts[a].at[k, 1], dst_ref=others[a].at[k],
            send_sem=xr_send.at[a, k], recv_sem=xr_recv.at[a, k],
            device_id={"ep": partner}, device_id_type=MESH,
        )

    def back_along(a, k):
        return pltpu.make_async_remote_copy(
            src_ref=parts[a].at[k, 0], dst_ref=outs[a].at[mine],
            send_sem=zr_send.at[a, k], recv_sem=zr_recv.at[a, k],
            device_id={"ep": 2 * behind(k) + half}, device_id_type=MESH,
        )

    def back_own(a):
        return pltpu.make_async_copy(parts[a].at[0, 0], outs[a].at[mine], lr_sem.at[a])

    def columns(c):
        return pl.ds(pl.multiple_of(c * piece, piece), piece)

    def tile(ref, k, c):
        return ref[k, :, :, columns(c)].reshape(2 * capacity, piece)

    def arrived(a, k):
        if k == 0:
            own(a).wait()
        across(a, k).wait_recv()

    zeros = jnp.zeros((2 * capacity, hidden_size), jnp.float32)

    def forward(k):
        arrived(0, k)

        def first(c, total):
            return total + jnp.dot(
                tile(f_rows, k, c), up_ref[columns(c), :], preferred_element_type=jnp.float32
            )

        pre = lax.fori_loop(0, pieces, first, zeros)
        hidden = (pre * jax.nn.sigmoid(pre)).astype(jnp.bfloat16)

        def second(c, carry):
            product = jnp.dot(hidden, down_ref[:, columns(c)], preferred_element_type=jnp.float32)
            f_part[k, :, :, columns(c)] = product.astype(jnp.bfloat16).reshape(2, capacity, piece)
            return carry

        lax.fori_loop(0, pieces, second, 0)

    def backward(k):
        arrived(1, k)
        arrived(2, k)

        def first(c, totals):
            pre, up = totals
            pre = pre + jnp.dot(
                tile(x_rows, k, c), up_ref[columns(c), :], preferred_element_type=jnp.float32
            )
            up = up + lax.dot_general(
                tile(g_rows, k, c), down_ref[:, columns(c)], NT, preferred_element_type=jnp.float32
            )
            return pre, up

        pre, up = lax.fori_loop(0, pieces, first, (zeros, zeros))
        hidden_grad = (silu_slope(pre) * up).astype(jnp.bfloat16)

        def second(c, carry):
            product = lax.dot_general(
                hidden_grad, up_ref[columns(c), :], NT, preferred_element_type=jnp.float32
            )
            b_part[k, :, :, columns(c)] = product.astype(jnp.bfloat16).reshape(2, capacity, piece)
            return carry

        lax.fori_loop(0, pieces, second, 0)

    def home(a, k):
        back_across(a, k).wait_recv()

        def add(c, carry):
            total = parts[a][k, 0, :, columns(c)].astype(jnp.float32) + others[a][
                k, :, columns(c)
            ].astype(jnp.float32)
            parts[a][k, 0, :, columns(c)] = total.astype(jnp.bfloat16)
            return carry

        lax.fori_loop(0, pieces, add, 0)
        if k == 0:
            back_own(a).start()
        else:
            back_along(a, k).start()

    across(0, 0).start()
    for k in range(1, experts):
        along(0, k).start()
    for a in (1, 2):
        across(a, 0).start()
    for k in range(1, experts):
        for a in (1, 2):
            along(a, k).start()
    for a in range(3):
        own(a).start()

    for k in range(1, experts):
        along(0, k).wait_recv()
        across(0, k).start()
    for k in range(1, experts):
        for a in (1, 2):
            along(a, k).wait_recv()
            across(a, k).start()
        forward(k - 1)
        if k > 1:
            back_across(0, k - 1).start()
    forward(experts - 1)
    back_across(0, experts - 1).start()
    back_across(0, 0).start()
    backward(0)
    for k in range(1, experts):
        backward(k)
        back_across(1, k).start()
        home(0, k)
    back_across(1, 0).start()
    home(0, 0)
    for k in range(1, experts):
        home(1, k)
    home(1, 0)

    for a in range(2):
        back_own(a).wait()
        for k in range(1, experts):
            back_along(a, k).wait()
        for k in range(experts):
            back_across(a, k).wait_send()
    for a in range(3):
        for k in range(1, experts):
            along(a, k).wait_send()
        for k in range(experts):
            across(a, k).wait_send()


def relay(f_in, x_in, g_in, w_up, w_down):
    experts, capacity, width = f_in.shape
    hidden_size = w_up.shape[1]
    kept = jnp.bfloat16
    any_space = pl.BlockSpec(memory_space=pl.ANY)
    vmem = pl.BlockSpec(memory_space=pltpu.VMEM)
    received = pltpu.VMEM((experts, 2, capacity, width), kept)
    exchanged = pltpu.VMEM((experts, capacity, width), kept)
    dma = pltpu.SemaphoreType.DMA
    row_count = 2 * experts * capacity
    result = jax.ShapeDtypeStruct((experts, capacity, width), kept)
    return pl.pallas_call(
        functools.partial(relay_kernel, experts),
        out_shape=(result, result),
        in_specs=[any_space] * 3 + [vmem] * 2,
        out_specs=(any_space, any_space),
        scratch_shapes=[received] * 5 + [exchanged] * 2 + [
            dma((3, experts)), dma((3, experts)), dma((3,)),
            dma((3, experts)), dma((3, experts)),
            dma((2, experts)), dma((2, experts)),
            dma((2, experts)), dma((2, experts)), dma((2,)),
        ],
        compiler_params=pltpu.CompilerParams(
            collective_id=0, has_side_effects=True, vmem_limit_bytes=60 * 1024 * 1024
        ),
        cost_estimate=pl.CostEstimate(
            flops=10 * row_count * width * hidden_size,
            bytes_accessed=10 * row_count * width,
            transcendentals=2 * row_count * hidden_size,
        ),
    )(f_in, x_in, g_in, w_up, w_down)


def on_device(
    fwd_tokens,
    fwd_routes,
    fwd_weights,
    bwd_tokens,
    bwd_grads,
    bwd_routes,
    bwd_weights,
    up_proj,
    down_proj,
):
    ep_count = lax.axis_size("ep")
    expert_count = ep_count // 2
    tok_rows = fwd_tokens.shape[1]
    feature_count = fwd_tokens.shape[2]
    route_count = fwd_routes.shape[2]
    capacity = 3 * tok_rows * route_count // ep_count
    slot_total = expert_count * capacity
    fwd_slots = slot_numbers(fwd_routes, expert_count, capacity)
    bwd_slots = slot_numbers(bwd_routes, expert_count, capacity)
    packed = pack_rows((fwd_tokens[0],), fwd_slots, slot_total) + pack_rows(
        (bwd_tokens[0], bwd_grads[0]), bwd_slots, slot_total
    )
    packed = [member.reshape(expert_count, capacity, feature_count) for member in packed]
    fwd_results, bwd_results = relay(*packed, up_proj[0], down_proj[0])
    fwd_out = combine_rows(
        fwd_tokens[0], fwd_results.reshape(slot_total, feature_count), fwd_slots, fwd_weights[0]
    )
    bwd_out = combine_rows(
        bwd_grads[0], bwd_results.reshape(slot_total, feature_count), bwd_slots, bwd_weights[0]
    )
    next_input = from_behind(fwd_out[None], "pp", 1)
    prev_grad = from_behind(bwd_out[None], "pp", -1)
    return (next_input, prev_grad)


def solution(mesh):
    placed = (
        P("pp", "ep", None),
        P("pp", "ep", None),
        P("pp", "ep", None),
        P("pp", "ep", None),
        P("pp", "ep", None),
        P("pp", "ep", None),
        P("pp", "ep", None),
        P("pp", None, "ep"),
        P("pp", "ep", None),
    )
    return jax.shard_map(
        on_device,
        mesh=mesh,
        in_specs=placed,
        out_specs=(P("pp", "ep", None), P("pp", "ep", None)),
        check_vma=False,
    )
```

time: 680 us -> 408 us (0.60)
  waiting for transfers between devices: 556 us -> 19.8 us
  Pallas kernels: 0 us -> 365 us
  starting transfers between devices: 26.4 us -> 0.12 us
  matrix products: 37.5 us -> 11.3 us
  local copies, waits for them, and re-layouts: 31.4 us -> 6.3 us
  other arithmetic: 26.8 us -> 3.92 us
    all_to_all x5 -> x0, waiting for transfers between devices: 543 us -> none  [the longest x3 336 us: pair_duplicate(): lax.all_to_all(as_sent(outgoing), 'ep', split_axis=0, concat_axis=0, tile...]
    pallas_call x0 -> x1, Pallas kernels: none -> 365 us  [relay(): pl.pallas_call(functools.partial(relay_kernel, experts), out_shape=(resul...]
    dot_general x3 -> x2, matrix products: 32.5 us -> 3.99 us  [combine_rows(): sums = jnp.dot(both, results, preferred_element_type=jnp.float32)]
    all_to_all x5 -> x0, starting transfers between devices: 26.4 us -> none  [the longest x3 16.8 us: pair_duplicate(): lax.all_to_all(as_sent(outgoing), 'ep', split_axis=0, concat_axis=0, tile...]
    reduce_sum x4 -> x2, other arithmetic: 22.5 us -> 0.27 us  [combine_rows(): table = jnp.sum(jnp.where(hot, route_weights[:, :, None], 0.0), axis=1)]
    convert_element_type x2 -> x0, local copies, waits for them, and re-layouts: 10.4 us -> none  [combine_rows(): picked = results[slots].astype(jnp.float32)]
    broadcast_in_dim x3 -> x0, local copies, waits for them, and re-layouts: 8.73 us -> none  [layout(): jnp.broadcast_to(member.reshape(expert_count, 1, capacity, feature_count)...]
    ppermute x2, waiting for transfers between devices: 12.8 us -> 19.8 us  [from_behind(): lax.ppermute(value, axis, [(i, (i + by) % size) for i in range(size)])]
  transfers between devices with their start and end apart: 7 -> 2, of which waited for: 6 -> 2; matrix products, arithmetic and copies ran while one was open for 12% -> 0% of each run, Pallas kernels for 0% -> 0%
where the time goes in v1:
time: 408 us
  Pallas kernels  365 us (89%)
  waiting for transfers between devices  19.8 us (5%)
  matrix products  11.3 us (3%)
  local copies, waits for them, and re-layouts  6.3 us (2%)
    pallas_call x1, Pallas kernels, relay(): pl.pallas_call(functools.partial(relay_kernel, experts), out_shape=(resul...  365 us
    ppermute x2, waiting for transfers between devices, from_behind(): lax.ppermute(value, axis, [(i, (i + by) % size) for i in range(size)])  19.8 us
  transfers between devices with their start and end apart: 2, of which 2 were waited for; matrix products, arithmetic and copies ran while one was open for 0% of the time, Pallas kernels for 0%

profile of v1, /device:TPU:0, one launch (start us, length us, event | category | flops | bytes accessed | tf_op | source)
XLA Modules:
  0.0 407.7 jit_solution(12723576922139275478)
XLA Ops:
  0.6 0.0 copy-start
  0.6 0.0 copy-start.1
  0.7 0.9 copy.37
  1.6 0.1 eq.107
  1.7 0.1 eq.103
  1.9 0.8 copy.31
  2.6 0.1 eq.96
  2.8 0.1 eq.92
  2.9 1.2 reduce-window.16
  4.2 0.1 slice.33
  4.2 0.1 copy.40
  4.4 0.1 copy.41
  4.5 0.1 add_bitcast_fusion
  4.6 0.1 reshape.91
  4.7 0.1 copy.42
  4.8 0.1 fusion.12
  4.9 0.0 copy-done
  5.0 2.5 convolution_convert_fusion.1
  7.4 0.0 copy-done.1
  7.4 0.0 copy-start.4
  7.4 0.0 copy-start.2
  7.4 2.4 convolution_convert_fusion
  9.8 1.2 reduce-window.14
  11.1 0.1 slice.32
  11.1 0.1 copy.34
  11.3 0.1 copy.35
  11.4 0.1 add_bitcast_fusion.1
  11.5 0.1 reshape.88
  11.6 0.1 copy.36
  11.7 0.1 fusion.11
  11.8 0.0 copy-done.4
  11.8 0.1 select_reduce_fusion
  12.0 0.0 copy-done.2
  12.0 2.5 convolution_convert_fusion.2
  14.5 365.4 %shard_map.104 = (bf16[4,96,3584]{2,1,0:T(8,128)(2,1)}, bf16[4,96,3584]{2,1,0:T(8,128)(2,1)}) custom-call(bf16[4,96,3584]{2,1,0:T(8,128)(2,1)} %bitcast.75, bf16[4,96,3584]{2,1,0:T(8,128)(2,1)} %bitcast.73, bf16[4,96,3584]{2,1,0:T(8,128)(2,1)} %bitcast.74, bf16[3584,512]{1,0:T(8,128)(2,1)} %bitcast.80, bf16[512,3584]{1,0:T(8,128)(2,1)} %bitcast.81), custom_call_target="tpu_custom_call" | custom-call | flops 14092861440 | bytes 27525120 | tf_op jit(solution)/shard_map/pallas_call | solution.py:263
  379.9 2.9 fusion.17
  382.8 0.0 copy-start.5
  382.8 0.0 copy-start.3
  382.8 0.3 fusion.3
  383.1 0.1 collective-permute-start.1
  383.2 0.3 copy-done.5
  383.5 0.1 select_reduce_fusion.1
  383.6 0.9 copy-done.3
  384.6 1.1 fusion.13
  385.7 0.3 fusion.2
  386.0 0.1 collective-permute-start
  386.1 14.0 %collective-permute-done.1 = bf16[1,128,3584]{2,1,0:T(8,128)(2,1)S(1)} collective-permute-done((bf16[1,128,3584]{2,1,0:T(8,128)(2,1)S(1)}, bf16[1,128,3584]{2,1,0:T(8,128)(2,1)S(1)}, u32[]{:S(2)}, u32[]{:S(2)}) %collective-permute-start.1) | collective-permute-done | bytes 917536 | tf_op jit(solution)/shard_map/ppermute | solution.py:17
  400.0 5.8 %collective-permute-done = bf16[1,128,3584]{2,1,0:T(8,128)(2,1)S(1)} collective-permute-done((bf16[1,128,3584]{2,1,0:T(8,128)(2,1)S(1)}, bf16[1,128,3584]{2,1,0:T(8,128)(2,1)S(1)}, u32[]{:S(2)}, u32[]{:S(2)}) %collective-permute-start) | collective-permute-done | bytes 917536 | tf_op jit(solution)/shard_map/ppermute | solution.py:17
  405.9 0.9 copy.49
  406.8 0.9 copy.50
  (12 shorter events, 0.2 us)
Async XLA Ops:
  0.6 4.3 %copy-start = (bf16[1,128,3584]{2,1,0:T(8,128)(2,1)S(1)}, bf16[1,128,3584]{2,1,0:T(8,128)(2,1)}, u32[]{:S(2)}) copy-start(bf16[1,128,3584]{2,1,0:T(8,128)(2,1)} %param.12) | copy-start | bytes 2752516
  0.6 6.8 %copy-start.1 = (bf16[1,128,3584]{2,1,0:T(8,128)(2,1)S(1)}, bf16[1,128,3584]{2,1,0:T(8,128)(2,1)}, u32[]{:S(2)}) copy-start(bf16[1,128,3584]{2,1,0:T(8,128)(2,1)} %param.13) | copy-start | bytes 2752516
  7.4 4.4 %copy-start.4 = (f32[1,128,2]{1,2,0:T(2,128)S(1)}, f32[1,128,2]{1,2,0:T(2,128)}, u32[]{:S(2)}) copy-start(f32[1,128,2]{1,2,0:T(2,128)} %param.15) | copy-start | bytes 3076
  7.4 4.6 %copy-start.2 = (bf16[1,128,3584]{2,1,0:T(8,128)(2,1)S(1)}, bf16[1,128,3584]{2,1,0:T(8,128)(2,1)}, u32[]{:S(2)}) copy-start(bf16[1,128,3584]{2,1,0:T(8,128)(2,1)} %param.9) | copy-start | bytes 2752516
  382.8 0.7 copy-start.5
  382.8 1.8 copy-start.3
  383.1 16.9 %collective-permute-start.1 = (bf16[1,128,3584]{2,1,0:T(8,128)(2,1)S(1)}, bf16[1,128,3584]{2,1,0:T(8,128)(2,1)S(1)}, u32[]{:S(2)}, u32[]{:S(2)}) collective-permute-start(bf16[1,128,3584]{2,1,0:T(8,128)(2,1)S(1)} %fusion.3), channel_id=1, source_target_pairs={{0,24},{8,0},{16,8},{24,16},{1,25},{9,1},{17,9},{25,17},{2,26},{10... | collective-permute-start | bytes 2752520 | tf_op jit(solution)/shard_map/ppermute | solution.py:17
  386.0 19.9 %collective-permute-start = (bf16[1,128,3584]{2,1,0:T(8,128)(2,1)S(1)}, bf16[1,128,3584]{2,1,0:T(8,128)(2,1)S(1)}, u32[]{:S(2)}, u32[]{:S(2)}) collective-permute-start(bf16[1,128,3584]{2,1,0:T(8,128)(2,1)S(1)} %fusion.2), channel_id=1, source_target_pairs={{0,8},{8,16},{16,24},{24,0},{1,9},{9,17},{17,25},{25,1},{2,10},{10... | collective-permute-start | bytes 2752520 | tf_op jit(solution)/shard_map/ppermute | solution.py:17

commit v2 on v1

--- a/solution.py
+++ b/solution.py
@@ -204,36 +204,36 @@
     across(0, 0).start()
     for k in range(1, experts):
         along(0, k).start()
+    for a in range(3):
+        own(a).start()
     for a in (1, 2):
         across(a, 0).start()
-    for k in range(1, experts):
-        for a in (1, 2):
-            along(a, k).start()
-    for a in range(3):
-        own(a).start()
 
     for k in range(1, experts):
         along(0, k).wait_recv()
         across(0, k).start()
-    for k in range(1, experts):
-        for a in (1, 2):
-            along(a, k).wait_recv()
-            across(a, k).start()
-        forward(k - 1)
-        if k > 1:
-            back_across(0, k - 1).start()
-    forward(experts - 1)
-    back_across(0, experts - 1).start()
+        along(1, k).start()
+    forward(0)
+    for k in range(1, experts):
+        along(1, k).wait_recv()
+        across(1, k).start()
+        along(2, k).start()
+        forward(k)
+        back_across(0, k).start()
+    for k in range(1, experts):
+        along(2, k).wait_recv()
+        across(2, k).start()
+        home(0, k)
     back_across(0, 0).start()
     backward(0)
     for k in range(1, experts):
         backward(k)
         back_across(1, k).start()
-        home(0, k)
+        if k > 1:
+            home(1, k - 1)
     back_across(1, 0).start()
     home(0, 0)
-    for k in range(1, experts):
-        home(1, k)
+    home(1, experts - 1)
     home(1, 0)
 
     for a in range(2):

time: 408 us -> 378 us (0.926)
  Pallas kernels: 365 us -> 336 us
    pallas_call x1, Pallas kernels: 365 us -> 336 us  [relay(): pl.pallas_call(functools.partial(relay_kernel, experts), out_shape=(resul...]
where the time goes in v2:
time: 378 us
  Pallas kernels  336 us (89%)
  waiting for transfers between devices  19.8 us (5%)
  matrix products  11.3 us (3%)
  local copies, waits for them, and re-layouts  6.16 us (2%)
  other arithmetic  3.93 us (1%)
    pallas_call x1, Pallas kernels, relay(): pl.pallas_call(functools.partial(relay_kernel, experts), out_shape=(resul...  336 us
    ppermute x2, waiting for transfers between devices, from_behind(): lax.ppermute(value, axis, [(i, (i + by) % size) for i in range(size)])  19.8 us
  transfers between devices with their start and end apart: 2, of which 2 were waited for; matrix products, arithmetic and copies ran while one was open for 0% of the time, Pallas kernels for 0%

profile of v2, /device:TPU:0, one launch (start us, length us, event | category | flops | bytes accessed | tf_op | source)
XLA Modules:
  0.0 378.2 jit_solution(7286251020658951590)
XLA Ops:
  0.6 0.0 copy-start
  0.6 0.0 copy-start.1
  0.7 0.9 copy.37
  1.6 0.1 eq.107
  1.7 0.1 eq.103
  1.9 0.8 copy.31
  2.6 0.1 eq.96
  2.8 0.1 eq.92
  2.9 1.2 reduce-window.16
  4.2 0.1 slice.33
  4.2 0.1 copy.40
  4.4 0.1 copy.41
  4.5 0.1 add_bitcast_fusion
  4.6 0.1 reshape.91
  4.7 0.1 copy.42
  4.8 0.1 fusion.12
  4.9 0.0 copy-done
  5.0 2.5 convolution_convert_fusion.1
  7.4 0.0 copy-done.1
  7.4 0.0 copy-start.4
  7.4 0.0 copy-start.2
  7.4 2.4 convolution_convert_fusion
  9.8 1.2 reduce-window.14
  11.1 0.1 slice.32
  11.1 0.1 copy.34
  11.3 0.1 copy.35
  11.4 0.1 add_bitcast_fusion.1
  11.5 0.1 reshape.88
  11.6 0.1 copy.36
  11.7 0.1 fusion.11
  11.8 0.0 copy-done.4
  11.8 0.1 select_reduce_fusion
  12.0 0.0 copy-done.2
  12.0 2.5 convolution_convert_fusion.2
  14.5 335.9 %shard_map.104 = (bf16[4,96,3584]{2,1,0:T(8,128)(2,1)}, bf16[4,96,3584]{2,1,0:T(8,128)(2,1)}) custom-call(bf16[4,96,3584]{2,1,0:T(8,128)(2,1)} %bitcast.75, bf16[4,96,3584]{2,1,0:T(8,128)(2,1)} %bitcast.73, bf16[4,96,3584]{2,1,0:T(8,128)(2,1)} %bitcast.74, bf16[3584,512]{1,0:T(8,128)(2,1)} %bitcast.80, bf16[512,3584]{1,0:T(8,128)(2,1)} %bitcast.81), custom_call_target="tpu_custom_call" | custom-call | flops 14092861440 | bytes 27525120 | tf_op jit(solution)/shard_map/pallas_call | solution.py:263
  350.4 2.9 fusion.17
  353.3 0.0 copy-start.5
  353.3 0.0 copy-start.3
  353.3 0.3 fusion.3
  353.6 0.2 collective-permute-start.1
  353.8 0.1 copy-done.5
  354.0 0.1 select_reduce_fusion.1
  354.2 0.9 copy-done.3
  355.1 1.1 fusion.13
  356.2 0.3 fusion.2
  356.5 0.1 collective-permute-start
  356.6 14.3 %collective-permute-done.1 = bf16[1,128,3584]{2,1,0:T(8,128)(2,1)S(1)} collective-permute-done((bf16[1,128,3584]{2,1,0:T(8,128)(2,1)S(1)}, bf16[1,128,3584]{2,1,0:T(8,128)(2,1)S(1)}, u32[]{:S(2)}, u32[]{:S(2)}) %collective-permute-start.1) | collective-permute-done | bytes 917536 | tf_op jit(solution)/shard_map/ppermute | solution.py:17
  370.9 5.5 %collective-permute-done = bf16[1,128,3584]{2,1,0:T(8,128)(2,1)S(1)} collective-permute-done((bf16[1,128,3584]{2,1,0:T(8,128)(2,1)S(1)}, bf16[1,128,3584]{2,1,0:T(8,128)(2,1)S(1)}, u32[]{:S(2)}, u32[]{:S(2)}) %collective-permute-start) | collective-permute-done | bytes 917536 | tf_op jit(solution)/shard_map/ppermute | solution.py:17
  376.4 0.9 copy.49
  377.3 0.9 copy.50
  (12 shorter events, 0.2 us)
Async XLA Ops:
  0.6 4.3 %copy-start = (bf16[1,128,3584]{2,1,0:T(8,128)(2,1)S(1)}, bf16[1,128,3584]{2,1,0:T(8,128)(2,1)}, u32[]{:S(2)}) copy-start(bf16[1,128,3584]{2,1,0:T(8,128)(2,1)} %param.12) | copy-start | bytes 2752516
  0.6 6.8 %copy-start.1 = (bf16[1,128,3584]{2,1,0:T(8,128)(2,1)S(1)}, bf16[1,128,3584]{2,1,0:T(8,128)(2,1)}, u32[]{:S(2)}) copy-start(bf16[1,128,3584]{2,1,0:T(8,128)(2,1)} %param.13) | copy-start | bytes 2752516
  7.4 4.4 %copy-start.4 = (f32[1,128,2]{1,2,0:T(2,128)S(1)}, f32[1,128,2]{1,2,0:T(2,128)}, u32[]{:S(2)}) copy-start(f32[1,128,2]{1,2,0:T(2,128)} %param.15) | copy-start | bytes 3076
  7.4 4.6 %copy-start.2 = (bf16[1,128,3584]{2,1,0:T(8,128)(2,1)S(1)}, bf16[1,128,3584]{2,1,0:T(8,128)(2,1)}, u32[]{:S(2)}) copy-start(bf16[1,128,3584]{2,1,0:T(8,128)(2,1)} %param.9) | copy-start | bytes 2752516
  353.3 0.7 copy-start.5
  353.3 1.8 copy-start.3
  353.6 17.2 %collective-permute-start.1 = (bf16[1,128,3584]{2,1,0:T(8,128)(2,1)S(1)}, bf16[1,128,3584]{2,1,0:T(8,128)(2,1)S(1)}, u32[]{:S(2)}, u32[]{:S(2)}) collective-permute-start(bf16[1,128,3584]{2,1,0:T(8,128)(2,1)S(1)} %fusion.3), channel_id=1, source_target_pairs={{0,24},{8,0},{16,8},{24,16},{1,25},{9,1},{17,9},{25,17},{2,26},{10... | collective-permute-start | bytes 2752520 | tf_op jit(solution)/shard_map/ppermute | solution.py:17
  356.5 19.9 %collective-permute-start = (bf16[1,128,3584]{2,1,0:T(8,128)(2,1)S(1)}, bf16[1,128,3584]{2,1,0:T(8,128)(2,1)S(1)}, u32[]{:S(2)}, u32[]{:S(2)}) collective-permute-start(bf16[1,128,3584]{2,1,0:T(8,128)(2,1)S(1)} %fusion.2), channel_id=1, source_target_pairs={{0,8},{8,16},{16,24},{24,0},{1,9},{9,17},{17,25},{25,1},{2,10},{10... | collective-permute-start | bytes 2752520 | tf_op jit(solution)/shard_map/ppermute | solution.py:17

commit v3 on v2

--- a/solution.py
+++ b/solution.py
@@ -12,64 +12,52 @@
 NN = (((1,), (0,)), ((), ()))
 
 
-def from_behind(value, axis, by):
-    size = lax.axis_size(axis)
-    return lax.ppermute(value, axis, [(i, (i + by) % size) for i in range(size)])
-
-
 def silu_slope(pre_act):
     sigmoid_value = jax.nn.sigmoid(pre_act)
     return sigmoid_value * (1.0 + pre_act * (1.0 - sigmoid_value))
 
 
-def slot_numbers(routes, expert_count, capacity):
-    chosen = routes[0]
-    tok_rows, route_count = chosen.shape
-    onehot = (
-        chosen[:, :, None] == jnp.arange(expert_count, dtype=jnp.int32)[None, None, :]
-    ).astype(jnp.int32)
-    flat_hot = onehot.reshape(tok_rows * route_count, expert_count)
-    earlier = jnp.cumsum(flat_hot, axis=0) - flat_hot
-    position = jnp.sum(earlier * flat_hot, axis=1).reshape(tok_rows, route_count)
-    return chosen * capacity + position
-
-
-def pack_rows(sources, slots, slot_total):
-    slot_table = jnp.sum(
-        (slots[:, :, None] == jnp.arange(slot_total, dtype=jnp.int32)[None, None, :]).astype(
-            jnp.bfloat16
-        ),
-        axis=1,
+def slot_numbers(chosen, expert_count, capacity):
+    batch, tok_rows, route_count = chosen.shape
+    flat = chosen.reshape(batch, tok_rows * route_count)
+    hot = flat[:, :, None] == jnp.arange(expert_count, dtype=jnp.int32)
+    order = jnp.arange(tok_rows * route_count, dtype=jnp.int32)
+    before = (order[None, :] < order[:, None]).astype(jnp.bfloat16)
+    earlier = jnp.einsum(
+        "ij,bje->bie", before, hot.astype(jnp.bfloat16), preferred_element_type=jnp.float32
     )
-    return tuple(
-        lax.dot_general(
-            slot_table, member, (((0,), (0,)), ((), ())), preferred_element_type=jnp.float32
-        ).astype(jnp.bfloat16)
-        for member in sources
-    )
-
-
-def combine_rows(residual, results, slots, route_weights):
-    slot_total = results.shape[0]
-    hot = slots[:, :, None] == jnp.arange(slot_total, dtype=jnp.int32)[None, None, :]
-    table = jnp.sum(jnp.where(hot, route_weights[:, :, None], 0.0), axis=1)
+    position = jnp.sum(jnp.where(hot, earlier, 0.0), axis=2).astype(jnp.int32)
+    return chosen * capacity + position.reshape(chosen.shape)
+
+
+def pick_table(slots, expert_count, capacity):
+    batch, tok_rows, _ = slots.shape
+    numbers = jnp.arange(expert_count * capacity, dtype=jnp.int32)[None, :, None]
+    first, second = slots[:, None, :, 0], slots[:, None, :, 1]
+    table = ((numbers == first) | (numbers == second)).astype(jnp.bfloat16)
+    return table.reshape(batch, expert_count, capacity, tok_rows)
+
+
+def weigh_table(slots, route_weights, slot_total):
+    hot = slots[:, :, :, None] == jnp.arange(slot_total, dtype=jnp.int32)
+    table = jnp.sum(jnp.where(hot, route_weights[:, :, :, None], 0.0), axis=2)
     high = lax.reduce_precision(table, 8, 7)
-    both = jnp.concatenate([high.astype(jnp.bfloat16), (table - high).astype(jnp.bfloat16)], axis=0)
-    sums = jnp.dot(both, results, preferred_element_type=jnp.float32)
-    rows = residual.shape[0]
-    return (residual.astype(jnp.float32) + sums[:rows] + sums[rows:]).astype(jnp.bfloat16)
+    return jnp.concatenate([high.astype(jnp.bfloat16), (table - high).astype(jnp.bfloat16)], axis=1)
 
 
 def relay_kernel(
-    experts, f_in, x_in, g_in, up_ref, down_ref, f_out, b_out,
-    f_rows, x_rows, g_rows, f_part, b_part, f_other, b_other,
-    z_send, z_recv, l_sem, x_send, x_recv, xr_send, xr_recv, zr_send, zr_recv, lr_sem,
+    experts, sections, f_tok, x_tok, g_tok, pick_ref, weigh_ref, up_ref, down_ref, next_ref, prev_ref,
+    f_rows, x_rows, g_rows, f_part, b_part, f_other, b_other, f_out, b_out, f_final, b_final,
+    z_send, z_recv, x_send, x_recv, xr_send, xr_recv, zr_send, zr_recv, lr_sem, p_send, p_recv,
 ):
     me = lax.axis_index("ep")
     mine = me // 2
     half = lax.rem(me, 2)
     partner = 2 * mine + 1 - half
-    capacity, width = f_in.shape[1], f_in.shape[2]
+    section = lax.axis_index("pp")
+    targets = (lax.rem(section + 1, sections), lax.rem(section + sections - 1, sections))
+    capacity, width = f_rows.shape[2], f_rows.shape[3]
+    tok_rows = f_tok.shape[0]
     piece = 512 if width % 512 == 0 else 128
     pieces = width // piece
     hidden_size = up_ref.shape[1]
@@ -86,27 +74,33 @@
         pl.semaphore_signal(
             barrier, inc=1, device_id={"ep": 2 * ahead(k) + half}, device_id_type=MESH
         )
-    pl.semaphore_wait(barrier, experts)
-
-    ins = (f_in, x_in, g_in)
+    for target in targets:
+        pl.semaphore_signal(barrier, inc=1, device_id={"pp": target}, device_id_type=MESH)
+    pl.semaphore_wait(barrier, experts + 2)
+
+    toks = (f_tok, x_tok, g_tok)
     rows = (f_rows, x_rows, g_rows)
     parts = (f_part, b_part)
     others = (f_other, b_other)
     outs = (f_out, b_out)
+    finals = (f_final, b_final)
+    ends = (next_ref, prev_ref)
+
+    def staged(a, k):
+        if k == 0:
+            return rows[a].at[0, 0]
+        return (f_part.at[k, 0], b_part.at[k, 0], b_part.at[k, 1])[a]
 
     def along(a, k):
         return pltpu.make_async_remote_copy(
-            src_ref=ins[a].at[ahead(k)], dst_ref=rows[a].at[k, 0],
+            src_ref=staged(a, k), dst_ref=rows[a].at[k, 0],
             send_sem=z_send.at[a, k], recv_sem=z_recv.at[a, k],
             device_id={"ep": 2 * ahead(k) + half}, device_id_type=MESH,
         )
 
-    def own(a):
-        return pltpu.make_async_copy(ins[a].at[mine], rows[a].at[0, 0], l_sem.at[a])
-
     def across(a, k):
         return pltpu.make_async_remote_copy(
-            src_ref=ins[a].at[mine] if k == 0 else rows[a].at[k, 0], dst_ref=rows[a].at[k, 1],
+            src_ref=rows[a].at[k, 0], dst_ref=rows[a].at[k, 1],
             send_sem=x_send.at[a, k], recv_sem=x_recv.at[a, k],
             device_id={"ep": partner}, device_id_type=MESH,
         )
@@ -135,9 +129,41 @@
         return ref[k, :, :, columns(c)].reshape(2 * capacity, piece)
 
     def arrived(a, k):
-        if k == 0:
-            own(a).wait()
         across(a, k).wait_recv()
+        if k > 0:
+            along(a, k).wait_send()
+
+    def pack(a, k):
+        table = pick_ref[min(a, 1), ahead(k)]
+        place = staged(a, k)
+
+        def put(c, carry):
+            picked = jnp.dot(table, toks[a][:, columns(c)], preferred_element_type=jnp.float32)
+            place[:, columns(c)] = picked.astype(jnp.bfloat16)
+            return carry
+
+        lax.fori_loop(0, pieces, put, 0)
+
+    def relayed(a, c):
+        place = pl.ds(c * piece, piece)
+        return pltpu.make_async_remote_copy(
+            src_ref=finals[a].at[:, place], dst_ref=ends[a].at[:, place],
+            send_sem=p_send.at[a, c], recv_sem=p_recv.at[a, c],
+            device_id={"pp": targets[a]}, device_id_type=MESH,
+        )
+
+    def combine(a):
+        back_own(a).wait()
+        for k in range(1, experts):
+            back_along(a, k).wait_recv()
+        residual = (f_tok, g_tok)[a]
+        for c in range(pieces):
+            place = pl.ds(c * piece, piece)
+            results = outs[a][:, :, place].reshape(experts * capacity, piece)
+            sums = jnp.dot(weigh_ref[a], results, preferred_element_type=jnp.float32)
+            total = residual[:, place].astype(jnp.float32) + sums[:tok_rows] + sums[tok_rows:]
+            finals[a][:, place] = total.astype(jnp.bfloat16)
+            relayed(a, c).start()
 
     zeros = jnp.zeros((2 * capacity, hidden_size), jnp.float32)
 
@@ -201,13 +227,15 @@
         else:
             back_along(a, k).start()
 
-    across(0, 0).start()
-    for k in range(1, experts):
+    for k in range(1, experts):
+        pack(0, k)
         along(0, k).start()
     for a in range(3):
-        own(a).start()
+        pack(a, 0)
+        across(a, 0).start()
     for a in (1, 2):
-        across(a, 0).start()
+        for k in range(1, experts):
+            pack(a, k)
 
     for k in range(1, experts):
         along(0, k).wait_recv()
@@ -233,43 +261,50 @@
             home(1, k - 1)
     back_across(1, 0).start()
     home(0, 0)
+    combine(0)
     home(1, experts - 1)
     home(1, 0)
+    combine(1)
 
     for a in range(2):
-        back_own(a).wait()
         for k in range(1, experts):
-            back_along(a, k).wait()
+            back_along(a, k).wait_send()
         for k in range(experts):
             back_across(a, k).wait_send()
     for a in range(3):
-        for k in range(1, experts):
-            along(a, k).wait_send()
         for k in range(experts):
             across(a, k).wait_send()
-
-
-def relay(f_in, x_in, g_in, w_up, w_down):
-    experts, capacity, width = f_in.shape
+    for a in range(2):
+        for c in range(pieces):
+            relayed(a, c).wait()
+
+
+def relay(f_tok, x_tok, g_tok, pick, weigh, w_up, w_down):
+    _, experts, capacity, tok_rows = pick.shape
+    width = f_tok.shape[1]
     hidden_size = w_up.shape[1]
+    sections = lax.axis_size("pp")
     kept = jnp.bfloat16
     any_space = pl.BlockSpec(memory_space=pl.ANY)
     vmem = pl.BlockSpec(memory_space=pltpu.VMEM)
     received = pltpu.VMEM((experts, 2, capacity, width), kept)
     exchanged = pltpu.VMEM((experts, capacity, width), kept)
+    final = pltpu.VMEM((tok_rows, width), kept)
     dma = pltpu.SemaphoreType.DMA
+    pieces = width // (512 if width % 512 == 0 else 128)
     row_count = 2 * experts * capacity
-    result = jax.ShapeDtypeStruct((experts, capacity, width), kept)
+    result = jax.ShapeDtypeStruct((tok_rows, width), kept)
     return pl.pallas_call(
-        functools.partial(relay_kernel, experts),
+        functools.partial(relay_kernel, experts, sections),
         out_shape=(result, result),
-        in_specs=[any_space] * 3 + [vmem] * 2,
+        in_specs=[vmem] * 7,
         out_specs=(any_space, any_space),
-        scratch_shapes=[received] * 5 + [exchanged] * 2 + [
-            dma((3, experts)), dma((3, experts)), dma((3,)),
+        scratch_shapes=[received] * 5 + [exchanged] * 4 + [final] * 2 + [
+            dma((3, experts)), dma((3, experts)),
             dma((3, experts)), dma((3, experts)),
             dma((2, experts)), dma((2, experts)),
             dma((2, experts)), dma((2, experts)), dma((2,)),
+            dma((2, pieces)), dma((2, pieces)),
         ],
         compiler_params=pltpu.CompilerParams(
             collective_id=0, has_side_effects=True, vmem_limit_bytes=60 * 1024 * 1024
@@ -279,7 +314,7 @@
             bytes_accessed=10 * row_count * width,
             transcendentals=2 * row_count * hidden_size,
         ),
-    )(f_in, x_in, g_in, w_up, w_down)
+    )(f_tok, x_tok, g_tok, pick, weigh, w_up, w_down)
 
 
 def on_device(
@@ -296,26 +331,16 @@
     ep_count = lax.axis_size("ep")
     expert_count = ep_count // 2
     tok_rows = fwd_tokens.shape[1]
-    feature_count = fwd_tokens.shape[2]
     route_count = fwd_routes.shape[2]
     capacity = 3 * tok_rows * route_count // ep_count
     slot_total = expert_count * capacity
-    fwd_slots = slot_numbers(fwd_routes, expert_count, capacity)
-    bwd_slots = slot_numbers(bwd_routes, expert_count, capacity)
-    packed = pack_rows((fwd_tokens[0],), fwd_slots, slot_total) + pack_rows(
-        (bwd_tokens[0], bwd_grads[0]), bwd_slots, slot_total
+    slots = slot_numbers(jnp.concatenate([fwd_routes, bwd_routes]), expert_count, capacity)
+    pick = pick_table(slots, expert_count, capacity)
+    weigh = weigh_table(slots, jnp.concatenate([fwd_weights, bwd_weights]), slot_total)
+    next_input, prev_grad = relay(
+        fwd_tokens[0], bwd_tokens[0], bwd_grads[0], pick, weigh, up_proj[0], down_proj[0]
     )
-    packed = [member.reshape(expert_count, capacity, feature_count) for member in packed]
-    fwd_results, bwd_results = relay(*packed, up_proj[0], down_proj[0])
-    fwd_out = combine_rows(
-        fwd_tokens[0], fwd_results.reshape(slot_total, feature_count), fwd_slots, fwd_weights[0]
-    )
-    bwd_out = combine_rows(
-        bwd_grads[0], bwd_results.reshape(slot_total, feature_count), bwd_slots, bwd_weights[0]
-    )
-    next_input = from_behind(fwd_out[None], "pp", 1)
-    prev_grad = from_behind(bwd_out[None], "pp", -1)
-    return (next_input, prev_grad)
+    return (next_input[None], prev_grad[None])
 
 
 def solution(mesh):

time: 378 us -> 360 us (0.952)
  waiting for transfers between devices: 19.8 us -> 0 us
  Pallas kernels: 336 us -> 349 us
  matrix products: 11.3 us -> 0.21 us
    ppermute x2 -> x0, waiting for transfers between devices: 19.8 us -> none  [from_behind(): lax.ppermute(value, axis, [(i, (i + by) % size) for i in range(size)])]
    pallas_call x1, Pallas kernels: 336 us -> 349 us  [relay(): pl.pallas_call(functools.partial(relay_kernel, experts, sections), out_sh...]
    dot_general x5 -> x1, matrix products: 11.3 us -> 0.21 us  [slot_numbers(): jnp.einsum('ij,bje->bie', before, hot.astype(jnp.bfloat16), preferred_ele...]
  transfers between devices with their start and end apart: 2 -> 0, of which waited for: 2 -> 0; matrix products, arithmetic and copies ran while one was open for 0% -> 0% of each run, Pallas kernels for 0% -> 0%
where the time goes in v3:
time: 360 us; the launch traced here: 359 us
  Pallas kernels  349 us (97%)
  local copies, waits for them, and re-layouts  6.18 us (2%)
    pallas_call x1, Pallas kernels, relay(): pl.pallas_call(functools.partial(relay_kernel, experts, sections), out_sh...  349 us

profile of v3, /device:TPU:0, one launch (start us, length us, event | category | flops | bytes accessed | tf_op | source)
XLA Modules:
  0.0 358.6 jit_solution(11975408152885820742)
XLA Ops:
  0.6 0.7 constant_dynamic-update-slice_fusion.1
  1.3 0.7 constant_dynamic-update-slice_fusion
  2.0 0.7 pad_maximum_fusion.1
  2.7 0.1 copy.27
  2.8 0.1 eq.74
  3.0 0.2 fusion.1
  3.2 0.1 convert_element_type.24
  3.4 0.1 copy.28
  3.4 0.8 or_convert_fusion.pick_ref
  4.3 0.2 select_reduce_fusion
  4.5 0.1 reduce-precision_convert_fusion
  4.5 0.8 pad_maximum_fusion.weigh_ref
  5.3 349.0 %shard_map.104 = (bf16[128,3584]{1,0:T(8,128)(2,1)}, bf16[128,3584]{1,0:T(8,128)(2,1)}) custom-call(bf16[128,3584]{1,0:T(8,128)(2,1)} %bitcast.24, bf16[128,3584]{1,0:T(8,128)(2,1)} %bitcast.25, bf16[128,3584]{1,0:T(8,128)(2,1)} %bitcast.26, bf16[2,4,96,128]{3,2,1,0:T(8,128)(2,1)} %or_convert_fusion.pick_ref, ...), custom_call_target="tpu_custom_call" | custom-call | flops 14092861440 | bytes 27525120 | tf_op jit(solution)/shard_map/pallas_call | solution.py:297
  354.3 2.2 copy.32
  356.5 2.2 copy.33
  (4 shorter events, 0.0 us)

commit v4 on v3

--- a/solution.py
+++ b/solution.py
@@ -105,22 +105,29 @@
             device_id={"ep": partner}, device_id_type=MESH,
         )
 
-    def back_across(a, k):
-        return pltpu.make_async_remote_copy(
-            src_ref=parts[a].at[k, 1], dst_ref=others[a].at[k],
-            send_sem=xr_send.at[a, k], recv_sem=xr_recv.at[a, k],
+    cuts = ((0, (pieces + 1) // 2), ((pieces + 1) // 2, pieces))
+
+    def span(h):
+        return pl.ds(cuts[h][0] * piece, (cuts[h][1] - cuts[h][0]) * piece)
+
+    def back_across(a, k, h):
+        return pltpu.make_async_remote_copy(
+            src_ref=parts[a].at[k, 1, :, span(h)], dst_ref=others[a].at[k, :, span(h)],
+            send_sem=xr_send.at[a, k, h], recv_sem=xr_recv.at[a, k, h],
             device_id={"ep": partner}, device_id_type=MESH,
         )
 
-    def back_along(a, k):
-        return pltpu.make_async_remote_copy(
-            src_ref=parts[a].at[k, 0], dst_ref=outs[a].at[mine],
-            send_sem=zr_send.at[a, k], recv_sem=zr_recv.at[a, k],
+    def back_along(a, k, h):
+        return pltpu.make_async_remote_copy(
+            src_ref=parts[a].at[k, 0, :, span(h)], dst_ref=outs[a].at[mine, :, span(h)],
+            send_sem=zr_send.at[a, k, h], recv_sem=zr_recv.at[a, k, h],
             device_id={"ep": 2 * behind(k) + half}, device_id_type=MESH,
         )
 
-    def back_own(a):
-        return pltpu.make_async_copy(parts[a].at[0, 0], outs[a].at[mine], lr_sem.at[a])
+    def back_own(a, h):
+        return pltpu.make_async_copy(
+            parts[a].at[0, 0, :, span(h)], outs[a].at[mine, :, span(h)], lr_sem.at[a, h]
+        )
 
     def columns(c):
         return pl.ds(pl.multiple_of(c * piece, piece), piece)
@@ -152,12 +159,12 @@
             device_id={"pp": targets[a]}, device_id_type=MESH,
         )
 
-    def combine(a):
-        back_own(a).wait()
+    def combine(a, h):
+        back_own(a, h).wait()
         for k in range(1, experts):
-            back_along(a, k).wait_recv()
+            back_along(a, k, h).wait_recv()
         residual = (f_tok, g_tok)[a]
-        for c in range(pieces):
+        for c in range(*cuts[h]):
             place = pl.ds(c * piece, piece)
             results = outs[a][:, :, place].reshape(experts * capacity, piece)
             sums = jnp.dot(weigh_ref[a], results, preferred_element_type=jnp.float32)
@@ -211,8 +218,8 @@
 
         lax.fori_loop(0, pieces, second, 0)
 
-    def home(a, k):
-        back_across(a, k).wait_recv()
+    def home(a, k, h):
+        back_across(a, k, h).wait_recv()
 
         def add(c, carry):
             total = parts[a][k, 0, :, columns(c)].astype(jnp.float32) + others[a][
@@ -221,11 +228,11 @@
             parts[a][k, 0, :, columns(c)] = total.astype(jnp.bfloat16)
             return carry
 
-        lax.fori_loop(0, pieces, add, 0)
+        lax.fori_loop(cuts[h][0], cuts[h][1], add, 0)
         if k == 0:
-            back_own(a).start()
+            back_own(a, h).start()
         else:
-            back_along(a, k).start()
+            back_along(a, k, h).start()
 
     for k in range(1, experts):
         pack(0, k)
@@ -247,30 +254,45 @@
         across(1, k).start()
         along(2, k).start()
         forward(k)
-        back_across(0, k).start()
+        for h in range(2):
+            back_across(0, k, h).start()
     for k in range(1, experts):
         along(2, k).wait_recv()
         across(2, k).start()
-        home(0, k)
-    back_across(0, 0).start()
+        for h in range(2):
+            home(0, k, h)
+    for h in range(2):
+        back_across(0, 0, h).start()
     backward(0)
     for k in range(1, experts):
         backward(k)
-        back_across(1, k).start()
+        back_across(1, k, 0).start()
         if k > 1:
-            home(1, k - 1)
-    back_across(1, 0).start()
-    home(0, 0)
-    combine(0)
-    home(1, experts - 1)
-    home(1, 0)
-    combine(1)
+            home(1, k - 1, 0)
+    back_across(1, 0, 0).start()
+    back_across(1, 1, 1).start()
+    for h in range(2):
+        home(0, 0, h)
+    for h in range(2):
+        combine(0, h)
+    for k in range(2, experts):
+        back_across(1, k, 1).start()
+    home(1, experts - 1, 0)
+    home(1, 0, 0)
+    back_across(1, 0, 1).start()
+    home(1, 1, 1)
+    combine(1, 0)
+    for k in range(2, experts):
+        home(1, k, 1)
+    home(1, 0, 1)
+    combine(1, 1)
 
     for a in range(2):
-        for k in range(1, experts):
-            back_along(a, k).wait_send()
-        for k in range(experts):
-            back_across(a, k).wait_send()
+        for h in range(2):
+            for k in range(1, experts):
+                back_along(a, k, h).wait_send()
+            for k in range(experts):
+                back_across(a, k, h).wait_send()
     for a in range(3):
         for k in range(experts):
             across(a, k).wait_send()
@@ -302,8 +324,8 @@
         scratch_shapes=[received] * 5 + [exchanged] * 4 + [final] * 2 + [
             dma((3, experts)), dma((3, experts)),
             dma((3, experts)), dma((3, experts)),
-            dma((2, experts)), dma((2, experts)),
-            dma((2, experts)), dma((2, experts)), dma((2,)),
+            dma((2, experts, 2)), dma((2, experts, 2)),
+            dma((2, experts, 2)), dma((2, experts, 2)), dma((2, 2)),
             dma((2, pieces)), dma((2, pieces)),
         ],
         compiler_params=pltpu.CompilerParams(

time: 360 us -> 351 us (0.975)
  Pallas kernels: 349 us -> 340 us
    pallas_call x1, Pallas kernels: 349 us -> 340 us  [relay(): pl.pallas_call(functools.partial(relay_kernel, experts, sections), out_sh...]
where the time goes in v4:
time: 351 us; the launch traced here: 349 us
  Pallas kernels  340 us (97%)
  local copies, waits for them, and re-layouts  6.18 us (2%)
    pallas_call x1, Pallas kernels, relay(): pl.pallas_call(functools.partial(relay_kernel, experts, sections), out_sh...  340 us

profile of v4, /device:TPU:0, one launch (start us, length us, event | category | flops | bytes accessed | tf_op | source)
XLA Modules:
  0.0 349.2 jit_solution(12012869475552381272)
XLA Ops:
  0.6 0.7 constant_dynamic-update-slice_fusion.1
  1.3 0.7 constant_dynamic-update-slice_fusion
  2.0 0.7 pad_maximum_fusion.1
  2.7 0.1 copy.27
  2.8 0.1 eq.74
  3.0 0.2 fusion.1
  3.2 0.1 convert_element_type.24
  3.4 0.1 copy.28
  3.4 0.8 or_convert_fusion.pick_ref
  4.3 0.2 select_reduce_fusion
  4.5 0.1 reduce-precision_convert_fusion
  4.5 0.8 pad_maximum_fusion.weigh_ref
  5.3 339.5 %shard_map.104 = (bf16[128,3584]{1,0:T(8,128)(2,1)}, bf16[128,3584]{1,0:T(8,128)(2,1)}) custom-call(bf16[128,3584]{1,0:T(8,128)(2,1)} %bitcast.24, bf16[128,3584]{1,0:T(8,128)(2,1)} %bitcast.25, bf16[128,3584]{1,0:T(8,128)(2,1)} %bitcast.26, bf16[2,4,96,128]{3,2,1,0:T(8,128)(2,1)} %or_convert_fusion.pick_ref, ...), custom_call_target="tpu_custom_call" | custom-call | flops 14092861440 | bytes 27525120 | tf_op jit(solution)/shard_map/pallas_call | solution.py:319
  344.8 2.2 copy.32
  347.0 2.2 copy.33
  (4 shorter events, 0.0 us)
